TPU v7x, 128 devices: a whole 4x4x4 slice. The times are simulated.
128 devices in a mesh: lat: 8 (over z, x_lo), lon: 16 (over x_hi, y, core).
Axes of the slice: x: 4 (x_hi: 2, x_lo: 2; x = x_hi * 2 + x_lo), y: 4, z: 4, core: 2. Of those that a mesh axis runs over, the one named last changes fastest.
Arguments:
- tokens: bfloat16 [96, 192, 2, 2048], P('lat', None, None, 'lon'), may hold values from -6 to 6
- upstream: bfloat16 [96, 192, 2, 2048], P('lat', 'lon'), may hold values from -6 to 6
- qkv_weight: bfloat16 [2048, 3072], P('lon'), may hold values from -1 to 1
- out_weight: bfloat16 [1024, 2048], P('lon'), may hold values from -0.1875 to 0.1875
Outputs:
- grad_tokens: bfloat16 [96, 192, 2, 2048], P('lat', None, None, 'lon')
- grad_qkv_w: float32 [8, 2048, 3072], P('lat', 'lon')
- grad_out_w: float32 [8, 1024, 2048], P('lat', 'lon')
All inputs are finite; a program needn't handle non-finite values.
Results may differ from a plain program's by a relative error of at most 0.017.
Values may be sent and summed in bfloat16 or wider, within the bound.
No kernel may reach another device: no remote copies, remote signals or barrier semaphores. Data moves between devices by JAX's collectives and lax.ppermute only.
A program may use at most 128 MiB of HBM per device.

v0:
```python
import jax
import jax.numpy as jnp
from jax import lax
from jax.sharding import PartitionSpec as P

HEADS = 16
HEAD_DIM = 64
WLAT = 12
WLON = 6
LEVELS = 2


NEG_FILL = -1e30
EPSILON = 1e-05


def passed_along(value, axis, by):
    devices = lax.axis_size(axis)
    return lax.ppermute(value, axis, [(i, (i + by) % devices) for i in range(devices)])


def attention_backward(qkv_flat, grad_att, labels):
    token_count = qkv_flat.shape[0]
    inner_width = HEADS * HEAD_DIM
    queries = qkv_flat[:, :inner_width].reshape(token_count, HEADS, HEAD_DIM)
    key_rows = qkv_flat[:, inner_width : 2 * inner_width].reshape(token_count, HEADS, HEAD_DIM)
    values = qkv_flat[:, 2 * inner_width :].reshape(token_count, HEADS, HEAD_DIM)
    score_scale = HEAD_DIM ** (-0.5)
    scores = (
        jnp.einsum("qhd,khd->hqk", queries, key_rows, preferred_element_type=jnp.float32)
        * score_scale
    )
    same_label = labels[:, None] == labels[None, :]
    scores = jnp.where(same_label[None], scores, NEG_FILL)
    top_score = jnp.max(scores, axis=-1, keepdims=True)
    expons = jnp.exp(scores - top_score)
    attention = expons / jnp.sum(expons, axis=-1, keepdims=True)
    attention_b = attention.astype(jnp.bfloat16)
    attended = jnp.einsum(
        "hqk,khd->qhd", attention_b, values, preferred_element_type=jnp.float32
    ).astype(jnp.bfloat16)
    grad_heads = grad_att.reshape(token_count, HEADS, HEAD_DIM)
    grad_probs = jnp.einsum("qhd,khd->hqk", grad_heads, values, preferred_element_type=jnp.float32)
    row_inner = jnp.sum(attention * grad_probs, axis=-1, keepdims=True)
    grad_scores = (attention * (grad_probs - row_inner) * score_scale).astype(jnp.bfloat16)
    grad_query = jnp.einsum(
        "hqk,khd->qhd", grad_scores, key_rows, preferred_element_type=jnp.float32
    ).astype(jnp.bfloat16)
    grad_key = jnp.einsum(
        "hqk,qhd->khd", grad_scores, queries, preferred_element_type=jnp.float32
    ).astype(jnp.bfloat16)
    grad_value = jnp.einsum(
        "hqk,qhd->khd", attention_b, grad_heads, preferred_element_type=jnp.float32
    ).astype(jnp.bfloat16)
    grad_qkv = jnp.concatenate(
        [
            grad_query.reshape(token_count, inner_width),
            grad_key.reshape(token_count, inner_width),
            grad_value.reshape(token_count, inner_width),
        ],
        axis=1,
    )
    return (attended.reshape(token_count, inner_width), grad_qkv)


def local_pass(rolled_in, rolled_grad, first_row, total_rows, qkv_full, out_full):
    row_count, col_count = (rolled_in.shape[0], rolled_in.shape[1])
    model_width = rolled_in.shape[-1]
    values_in = rolled_in.reshape(-1, model_width).astype(jnp.float32)
    average = jnp.mean(values_in, axis=-1, keepdims=True)
    centred = values_in - average
    inverse = lax.rsqrt(jnp.mean(centred * centred, axis=-1, keepdims=True) + EPSILON)
    normal_full = centred * inverse
    normed = normal_full.astype(jnp.bfloat16)
    qkv_flat = jnp.dot(normed, qkv_full, preferred_element_type=jnp.float32).astype(jnp.bfloat16)
    grad_flat = rolled_grad.reshape(-1, model_width)
    grad_att = lax.dot_general(
        grad_flat, out_full, (((1,), (1,)), ((), ())), preferred_element_type=jnp.float32
    ).astype(jnp.bfloat16)
    local_rows = jnp.arange(row_count, dtype=jnp.int32)
    row_ids = first_row + local_rows
    groups = (row_ids >= total_rows - WLAT // 2).astype(jnp.int32)
    col_ids = jnp.arange(col_count, dtype=jnp.int32)
    window_ids = (local_rows // WLAT)[:, None] * (col_count // WLON) + (col_ids // WLON)[None, :]
    label_grid = window_ids * 2 + groups[:, None]
    labels = jnp.broadcast_to(label_grid[:, :, None], (row_count, col_count, LEVELS)).reshape(-1)
    attended, grad_qkv = attention_backward(qkv_flat, grad_att, labels)
    grad_normal = lax.dot_general(
        grad_qkv, qkv_full, (((1,), (1,)), ((), ())), preferred_element_type=jnp.float32
    )
    mean_one = jnp.mean(grad_normal, axis=-1, keepdims=True)
    mean_two = jnp.mean(grad_normal * normal_full, axis=-1, keepdims=True)
    grad_rolled = (
        (inverse * (grad_normal - mean_one - normal_full * mean_two))
        .astype(jnp.bfloat16)
        .reshape(rolled_in.shape)
    )
    return (grad_rolled, normed, grad_qkv, attended, grad_flat)


def local(tokens, upstream, qkv_weight, out_weight):
    half_lat = WLAT // 2
    half_lon = WLON // 2
    row_count = upstream.shape[0]
    tiled = lax.all_to_all(tokens, "lon", split_axis=1, concat_axis=3, tiled=True)
    lat_rims = passed_along((tiled[:half_lat], upstream[:half_lat]), "lat", -1)
    tiled = jnp.concatenate([tiled[half_lat:], lat_rims[0]], axis=0)
    rolled_grad = jnp.concatenate([upstream[half_lat:], lat_rims[1]], axis=0)
    lon_rims = passed_along((tiled[:, :half_lon], rolled_grad[:, :half_lon]), "lon", -1)
    rolled_in = jnp.concatenate([tiled[:, half_lon:], lon_rims[0]], axis=1)
    rolled_grad = jnp.concatenate([rolled_grad[:, half_lon:], lon_rims[1]], axis=1)
    qkv_full, out_full = (
        lax.all_gather(qkv_weight, "lon", axis=0, tiled=True),
        lax.all_gather(out_weight, "lon", axis=0, tiled=True),
    )
    first_row = lax.axis_index("lat") * row_count
    total_rows = row_count * lax.axis_size("lat")
    grad_rolled, normed, grad_qkv, attended, grad_flat = local_pass(
        rolled_in, rolled_grad, first_row, total_rows, qkv_full, out_full
    )
    term_qkv = lax.dot_general(
        normed, grad_qkv, (((0,), (0,)), ((), ())), preferred_element_type=jnp.float32
    )
    term_out = lax.dot_general(
        attended, grad_flat, (((0,), (0,)), ((), ())), preferred_element_type=jnp.float32
    )
    grad_qkv_w, grad_out_w = (
        lax.psum_scatter(
            term_qkv.astype(jnp.bfloat16), "lon", scatter_dimension=0, tiled=True
        ).astype(jnp.float32),
        lax.psum_scatter(
            term_out.astype(jnp.bfloat16), "lon", scatter_dimension=0, tiled=True
        ).astype(jnp.float32),
    )
    carried = grad_rolled
    previous = passed_along(carried[-half_lat:], "lat", 1)
    carried = jnp.concatenate([previous, carried[:-half_lat]], axis=0)
    edge_cols = passed_along(carried[:, -half_lon:], "lon", 1)
    carried = jnp.concatenate([edge_cols, carried[:, :-half_lon]], axis=1)
    carried = (upstream.astype(jnp.float32) + carried.astype(jnp.float32)).astype(jnp.bfloat16)
    result = lax.all_to_all(carried, "lon", split_axis=3, concat_axis=1, tiled=True)
    return (result, grad_qkv_w[None], grad_out_w[None])


def solution(mesh):
    return jax.shard_map(
        local,
        mesh=mesh,
        in_specs=(
            P("lat", None, None, "lon"),
            P("lat", "lon", None, None),
            P("lon", None),
            P("lon", None),
        ),
        out_specs=(P("lat", None, None, "lon"), P("lat", "lon", None), P("lat", "lon", None)),
        check_vma=False,
    )
```

profile of v0, /device:TPU:1, one launch (start us, length us, event | category | flops | bytes accessed | tf_op | source)
XLA Modules:
  0.0 410.6 jit_solution(7835908792316701684)
XLA Ops:
  7.2 0.7 all-gather.3.cloned.1.call-update
  7.9 0.7 all-gather.5.cloned.1.call-update
  8.7 3.2 copy.86
  11.8 8.4 %all-to-all-start = ((bf16[12,192,2,128]{3,2,0,1:T(2,128)(2,1)}), bf16[12,192,2,128]{3,2,0,1:T(2,128)(2,1)S(1)}, u32[]{:S(2)}, u32[]{:S(2)}) async-start(bf16[12,192,2,128]{3,2,0,1:T(2,128)(2,1)} %copy.86), calls=%async_computation | async-start | bytes 2359296 | tf_op jit(solution)/shard_map/all_to_all | solution.py:105
  20.3 2.1 fusion.52
  22.4 3.8 collective-permute-start.2
  26.6 20.6 %all-to-all-done = bf16[12,192,2,128]{3,2,0,1:T(2,128)(2,1)S(1)} async-done(((bf16[12,192,2,128]{3,2,0,1:T(2,128)(2,1)}), bf16[12,192,2,128]{3,2,0,1:T(2,128)(2,1)S(1)}, u32[]{:S(2)}, u32[]{:S(2)}) %all-to-all-start) | async-done | bytes 1179680 | tf_op jit(solution)/shard_map/all_to_all | solution.py:105
  47.2 0.8 fusion.51
  48.1 1.0 slice.60
  49.1 4.0 collective-permute-start
  53.0 0.8 broadcast_compare_fusion
  53.8 1.8 collective-permute-done.2
  55.7 2.0 pad_maximum_fusion.4
  57.7 0.8 collective-permute-start.3
  58.8 0.5 constant_dynamic-update-slice_fusion.1
  59.3 13.8 %collective-permute-done = bf16[6,12,2,2048]{3,2,1,0:T(2,128)(2,1)} collective-permute-done((bf16[6,12,2,2048]{3,2,1,0:T(2,128)(2,1)}, bf16[6,12,2,2048]{3,2,1,0:T(2,128)(2,1)}, u32[]{:S(2)}, u32[]{:S(2)}) %collective-permute-start) | collective-permute-done | bytes 589856 | tf_op jit(solution)/shard_map/ppermute | solution.py:19
  73.1 1.6 constant_dynamic-update-slice_fusion
  74.8 1.1 slice.79
  75.8 2.0 collective-permute-start.1
  77.8 2.1 fusion.33
  80.0 2.5 pad_maximum_fusion.1
  82.5 1.3 reshape.197
  83.7 1.8 slice.78
  85.5 0.3 collective-permute-done.1
  85.9 1.3 fusion.47
  87.3 2.1 multiply_reduce_fusion.2
  89.6 2.7 maximum_convert_fusion
  92.2 3.4 reshape.204
  95.6 24.5 %all-gather.3.cloned.1.call-done = bf16[2048,3072]{1,0:T(8,128)(2,1)} async-done(((bf16[128,3072]{1,0:T(8,128)(2,1)}), bf16[2048,3072]{1,0:T(8,128)(2,1)}) %all-gather.3.cloned.1.call-update) | async-done | bytes 12582928 | tf_op jit(solution)/shard_map/all_gather | solution.py:113
  120.1 8.5 %convolution_convert_fusion.1 = bf16[288,3072]{1,0:T(8,128)(2,1)S(1)} fusion(bf16[2048,3072]{1,0:T(8,128)(2,1)} %all-gather.3.cloned.1.call-done, f32[288,2048]{1,0:T(8,128)S(1)} %reshape.204, f32[288]{0:T(512)S(1)} %div.42, f32[288]{0:T(512)S(1)} %rsqrt.12), kind=kOutput, calls=%fused_computation.9 | convolution fusion | flops 3626532864 | bytes 16713984 | tf_op jit(solution)/shard_map/dot_general | solution.py:75
  128.6 1.2 fusion.49
  129.9 2.2 copy.89
  132.1 2.2 copy.90
  134.3 2.2 copy.92
  136.6 7.3 %fusion.53 = (f32[16,288]{1,0:T(8,128)}, f32[16,288,288]{1,2,0:T(8,128)}) fusion(pred[288,288]{0,1:T(8,128)(4,1)} %broadcast_compare_fusion, bf16[288,16,64]{0,2,1:T(8,128)(2,1)} %bitcast.63, bf16[288,16,64]{0,2,1:T(8,128)(2,1)} %bitcast.61), kind=kOutput, calls=%fused_computation.75 | convolution fusion | flops 175178016 | bytes 6589440 | tf_op jit(solution)/shard_map/sub | solution.py:36
  143.8 4.1 %fusion.23 = bf16[16,64,288]{2,1,0:T(8,128)(2,1)S(1)} fusion(bf16[288,16,64]{0,2,1:T(8,128)(2,1)} %bitcast.56, f32[16,288,288]{1,2,0:T(8,128)} %get-tuple-element.15, f32[16,288]{1,0:T(8,128)} %get-tuple-element.14), kind=kOutput, calls=%fused_computation.29 | convolution fusion | flops 172818432 | bytes 6506496 | tf_op jit(solution)/shard_map/hqk,khd->qhd/dot_general | solution.py:39
  148.0 4.3 %convolution_convert_fusion.2 = bf16[1024,2048]{1,0:T(8,128)(2,1)} fusion(bf16[288,1024]{0,1:T(8,128)(2,1)S(1)} %bitcast.71, bf16[288,2048]{1,0:T(8,128)(2,1)S(1)} %copy-done.2), kind=kOutput, calls=%fused_computation.10 | convolution fusion | flops 1210056704 | bytes 5963776 | tf_op jit(solution)/shard_map/dot_general | solution.py:124
  152.3 0.5 reduce-scatter.3.cloned.1.call-start
  152.8 28.0 %all-gather.5.cloned.1.call-done = bf16[1024,2048]{1,0:T(8,128)(2,1)} async-done(((bf16[64,2048]{1,0:T(8,128)(2,1)}), bf16[1024,2048]{1,0:T(8,128)(2,1)}) %all-gather.5.cloned.1.call-update) | async-done | bytes 4194320 | tf_op jit(solution)/shard_map/all_gather | solution.py:114
  180.8 4.8 %convolution_convert_fusion.3 = bf16[288,1024]{1,0:T(8,128)(2,1)} fusion(bf16[288,2048]{1,0:T(8,128)(2,1)} %reshape.197, bf16[1024,2048]{1,0:T(8,128)(2,1)} %all-gather.5.cloned.1.call-done), kind=kOutput, calls=%fused_computation.32 | convolution fusion | flops 1208254464 | bytes 5963776 | tf_op jit(solution)/shard_map/dot_general | solution.py:77
  185.6 2.2 copy.91
  187.8 5.4 %fusion.54 = f32[16,288,288]{1,2,0:T(8,128)} fusion(bf16[288,16,64]{0,2,1:T(8,128)(2,1)} %bitcast.58, bf16[288,16,64]{0,2,1:T(8,128)(2,1)} %bitcast.57), kind=kOutput, calls=%fused_computation.76 | convolution fusion | flops 169869312 | bytes 6488064 | tf_op jit(solution)/shard_map/qhd,khd->hqk/dot_general | solution.py:43
  193.3 13.8 %fusion.26 = bf16[16,64,288]{2,1,0:T(8,128)(2,1)} fusion(bf16[288,16,64]{0,2,1:T(8,128)(2,1)} %bitcast.62, f32[16,288,288]{1,2,0:T(8,128)} %fusion.54, f32[16,288,288]{1,2,0:T(8,128)} %get-tuple-element.15, f32[16,288]{1,0:T(8,128)} %get-tuple-element.14), kind=kOutput, calls=%fused_computation.30 | convolution fusion | flops 179458848 | bytes 11814912 | tf_op jit(solution)/shard_map/hqk,khd->qhd/dot_general | solution.py:46
  207.0 12.3 %fusion.29 = bf16[16,64,288]{2,1,0:T(8,128)(2,1)} fusion(bf16[288,16,64]{0,2,1:T(8,128)(2,1)} %bitcast.64, f32[16,288,288]{1,2,0:T(8,128)} %fusion.54, f32[16,288,288]{1,2,0:T(8,128)} %get-tuple-element.15, f32[16,288]{1,0:T(8,128)} %get-tuple-element.14), kind=kOutput, calls=%fused_computation.31 | convolution fusion | flops 179458848 | bytes 11814912 | tf_op jit(solution)/shard_map/hqk,qhd->khd/dot_general | solution.py:49
  219.4 4.6 %fusion.20 = bf16[16,64,288]{2,1,0:T(8,128)(2,1)S(1)} fusion(bf16[288,16,64]{0,2,1:T(8,128)(2,1)} %bitcast.59, f32[16,288,288]{1,2,0:T(8,128)} %get-tuple-element.15, f32[16,288]{1,0:T(8,128)} %get-tuple-element.14), kind=kOutput, calls=%fused_computation.28 | convolution fusion | flops 172818432 | bytes 6506496 | tf_op jit(solution)/shard_map/hqk,qhd->khd/dot_general | solution.py:52
  224.0 0.9 copy-done.5
  224.9 11.8 %convolution_convert_fusion = bf16[2048,3072]{1,0:T(8,128)(2,1)} fusion(bf16[288,1024]{0,1:T(8,128)(2,1)S(1)} %bitcast.69, bf16[288,1024]{0,1:T(8,128)(2,1)S(1)} %bitcast.68, bf16[288,1024]{0,1:T(8,128)(2,1)S(1)} %bitcast.66, f32[288,2048]{1,0:T(8,128)S(1)} %reshape.204, f32[288]{0:T(512)S(1)} %div.42, f32[288]{0:T(512)S(1)} %rsqrt.12), kind=kOutput, calls=%fused_computation.2 | convolution fusion | flops 3637248000 | bytes 16713984 | tf_op jit(solution)/shard_map/dot_general | solution.py:121
  236.7 10.8 %fusion.48 = (f32[288]{0:T(512)S(1)}, f32[288]{0:T(512)S(1)}, f32[288,2048]{1,0:T(8,128)S(1)}) fusion(f32[288]{0:T(512)S(1)} %rsqrt.12, f32[288,2048]{1,0:T(8,128)S(1)} %reshape.204, f32[288]{0:T(512)S(1)} %div.42, bf16[2048,3072]{1,0:T(8,128)(2,1)} %all-gather.3.cloned.1.call-done, bf16[288,1024]{0,1:T(8,128)(2,1)} %bitcast.70, ...), kind=kOutput, calls=%fused_computation.70 | convolution fusion | flops 3632135680 | bytes 19075584 | tf_op jit(solution)/shard_map/dot_general | solution.py:88
  247.5 0.7 multiply_convert_fusion.1
  248.4 0.4 slice.71
  248.8 1.1 copy.96
  249.9 0.5 collective-permute-start.4
  250.4 0.4 slice.73
  250.8 20.6 %collective-permute-done.4 = bf16[6,12,2,2048]{3,1,2,0:T(8,128)(2,1)S(1)} collective-permute-done((bf16[6,12,2,2048]{3,1,2,0:T(8,128)(2,1)}, bf16[6,12,2,2048]{3,1,2,0:T(8,128)(2,1)S(1)}, u32[]{:S(2)}, u32[]{:S(2)}) %collective-permute-start.4) | collective-permute-done | bytes 589856 | tf_op jit(solution)/shard_map/ppermute | solution.py:19
  272.1 2.2 collective-permute-start.5
  274.3 4.7 %collective-permute-done.5 = bf16[12,3,2,2048]{3,0,2,1:T(8,128)(2,1)S(1)} collective-permute-done((bf16[12,3,2,2048]{3,0,2,1:T(8,128)(2,1)S(1)}, bf16[12,3,2,2048]{3,0,2,1:T(8,128)(2,1)S(1)}, u32[]{:S(2)}, u32[]{:S(2)}) %collective-permute-start.5) | collective-permute-done | bytes 294944 | tf_op jit(solution)/shard_map/ppermute | solution.py:19
  279.3 1.1 add_convert_fusion
  280.4 23.7 %copy.100 = bf16[12,12,2,2048]{1,0,2,3:T(8,128)(2,1)} copy(bf16[12,12,2,2048]{3,1,2,0:T(8,128)(2,1)S(1)} %add_convert_fusion) | data formatting | bytes 2359296 | tf_op jit(solution)/shard_map/convert_element_type | solution.py:140
  304.0 19.0 %reshape.207 = bf16[16,2,18432]{2,1,0:T(2,128)(2,1)S(1)} reshape(bf16[2048,2,12,12]{3,2,1,0:T(8,128)(2,1)} %bitcast.52) | data formatting | bytes 2359296
  323.0 39.1 %all_to_all.33 = bf16[16,2,18432]{2,1,0:T(2,128)(2,1)S(1)} all-to-all(bf16[16,2,18432]{2,1,0:T(2,128)(2,1)S(1)} %reshape.207), channel_id=1, replica_groups=mesh['lat'=8,'lon'=16] {'lon'}, dimensions={0} | all-to-all | bytes 2359296 | tf_op jit(solution)/shard_map/all_to_all | solution.py:141
  362.1 17.6 %reshape.208 = bf16[2048,2,12,12]{3,2,1,0:T(8,128)(2,1)} reshape(bf16[16,2,18432]{2,1,0:T(2,128)(2,1)S(1)} %all_to_all.33) | data formatting | bytes 2359296
  379.7 19.9 %copy.101 = bf16[12,16,12,2,128]{4,3,2,1,0:T(2,128)(2,1)} copy(bf16[12,16,12,2,128]{2,0,3,4,1:T(8,128)(2,1)} %bitcast.53) | data formatting | bytes 2359296 | tf_op jit(solution)/shard_map/all_to_all | solution.py:141
  399.6 1.8 bitcast_convert_fusion.1
  401.4 2.4 bitcast_convert_fusion
  (39 shorter events, 2.3 us)
Async XLA Ops:
  7.2 112.9 %all-gather.3.cloned.1.call-start = ((), (), s32[]{:S(2)}) async-start(), calls=%async_computation.4 | async-start | bytes 13369344 | tf_op jit(solution)/shard_map/all_gather | solution.py:113
  7.9 172.9 %all-gather.5.cloned.1.call-start = ((), (), s32[]{:S(2)}) async-start(), calls=%async_computation.5 | async-start | bytes 4456448 | tf_op jit(solution)/shard_map/all_gather | solution.py:114
  8.6 11.7 %copy-start = (bf16[12,12,2,2048]{3,2,1,0:T(2,128)(2,1)S(1)}, bf16[12,12,2,2048]{3,2,1,0:T(2,128)(2,1)}, u32[]{:S(2)}) copy-start(bf16[12,12,2,2048]{3,2,1,0:T(2,128)(2,1)} %param.5) | copy-start | bytes 3538948
  11.8 35.3 %all-to-all-start = ((bf16[12,192,2,128]{3,2,0,1:T(2,128)(2,1)}), bf16[12,192,2,128]{3,2,0,1:T(2,128)(2,1)S(1)}, u32[]{:S(2)}, u32[]{:S(2)}) async-start(bf16[12,192,2,128]{3,2,0,1:T(2,128)(2,1)} %copy.86), calls=%async_computation | async-start | bytes 2359296 | tf_op jit(solution)/shard_map/all_to_all | solution.py:105
  20.3 379.3 %reduce-scatter.5.cloned.1.call-start = ((), (), s32[]{:S(2)}) async-start(), calls=%async_computation.7 | async-start | bytes 4456448 | tf_op jit(solution)/shard_map/reduce_scatter | solution.py:131
  22.4 33.3 %collective-permute-start.2 = (bf16[6,12,2,2048]{3,2,1,0:T(2,128)(2,1)}, bf16[6,12,2,2048]{3,2,1,0:T(2,128)(2,1)}, u32[]{:S(2)}, u32[]{:S(2)}) collective-permute-start(bf16[6,12,2,2048]{3,2,1,0:T(2,128)(2,1)} %get-tuple-element.13), channel_id=1, source_target_pairs={{0,112},{16,0},{32,16},{48,32},{64,48},{80,64},{96,80},{112,96},{1... | collective-permute-start | bytes 1769480 | tf_op jit(solution)/shard_map/ppermute | solution.py:19
  49.1 24.0 %collective-permute-start = (bf16[6,12,2,2048]{3,2,1,0:T(2,128)(2,1)}, bf16[6,12,2,2048]{3,2,1,0:T(2,128)(2,1)}, u32[]{:S(2)}, u32[]{:S(2)}) collective-permute-start(bf16[6,12,2,2048]{3,2,1,0:T(2,128)(2,1)} %slice.60), channel_id=1, source_target_pairs={{0,112},{16,0},{32,16},{48,32},{64,48},{80,64},{96,80},{112,96},{1... | collective-permute-start | bytes 1769480 | tf_op jit(solution)/shard_map/ppermute | solution.py:19
  57.7 22.3 %collective-permute-start.3 = (bf16[12,3,2,2048]{3,2,1,0:T(2,128)(2,1)}, bf16[12,3,2,2048]{3,2,1,0:T(2,128)(2,1)}, u32[]{:S(2)}, u32[]{:S(2)}) collective-permute-start(bf16[12,3,2,2048]{3,2,1,0:T(2,128)(2,1)} %pad_maximum_fusion.4), channel_id=1, source_target_pairs={{0,15},{1,0},{2,1},{3,2},{4,3},{5,4},{6,5},{7,6},{8,7},{9,8},{10,9... | collective-permute-start | bytes 884744 | tf_op jit(solution)/shard_map/ppermute | solution.py:19
  74.7 1.1 copy-start.1
  75.8 10.0 %collective-permute-start.1 = (bf16[12,3,2,2048]{3,2,1,0:T(2,128)(2,1)}, bf16[12,3,2,2048]{3,2,1,0:T(2,128)(2,1)S(1)}, u32[]{:S(2)}, u32[]{:S(2)}) collective-permute-start(bf16[12,3,2,2048]{3,2,1,0:T(2,128)(2,1)} %slice.79), channel_id=1, source_target_pairs={{0,15},{1,0},{2,1},{3,2},{4,3},{5,4},{6,5},{7,6},{8,7},{9,8},{10,9... | collective-permute-start | bytes 884744 | tf_op jit(solution)/shard_map/ppermute | solution.py:19
  143.8 4.1 %copy-start.2 = (bf16[288,2048]{1,0:T(8,128)(2,1)S(1)}, bf16[288,2048]{1,0:T(8,128)(2,1)}, u32[]{:S(2)}) copy-start(bf16[288,2048]{1,0:T(8,128)(2,1)} %reshape.197) | copy-start | bytes 3538948
  152.3 249.1 %reduce-scatter.3.cloned.1.call-start = ((), (), s32[]{:S(2)}) async-start(), calls=%async_computation.6 | async-start | bytes 13369344 | tf_op jit(solution)/shard_map/reduce_scatter | solution.py:128
  219.4 5.5 %copy-start.3 = (bf16[16,64,288]{2,1,0:T(8,128)(2,1)S(1)}, bf16[16,64,288]{2,1,0:T(8,128)(2,1)}, u32[]{:S(2)}) copy-start(bf16[16,64,288]{2,1,0:T(8,128)(2,1)} %fusion.26) | copy-start | bytes 1769476
  219.4 5.5 %copy-start.4 = (bf16[16,64,288]{2,1,0:T(8,128)(2,1)S(1)}, bf16[16,64,288]{2,1,0:T(8,128)(2,1)}, u32[]{:S(2)}) copy-start(bf16[16,64,288]{2,1,0:T(8,128)(2,1)} %fusion.29) | copy-start | bytes 1769476
  224.0 0.9 copy-start.5
  249.9 21.5 %collective-permute-start.4 = (bf16[6,12,2,2048]{3,1,2,0:T(8,128)(2,1)}, bf16[6,12,2,2048]{3,1,2,0:T(8,128)(2,1)S(1)}, u32[]{:S(2)}, u32[]{:S(2)}) collective-permute-start(bf16[6,12,2,2048]{3,1,2,0:T(8,128)(2,1)} %copy.96), channel_id=1, source_target_pairs={{0,16},{16,32},{32,48},{48,64},{64,80},{80,96},{96,112},{112,0},{1... | collective-permute-start | bytes 1769480 | tf_op jit(solution)/shard_map/ppermute | solution.py:19
  272.1 6.9 %collective-permute-start.5 = (bf16[12,3,2,2048]{3,0,2,1:T(8,128)(2,1)S(1)}, bf16[12,3,2,2048]{3,0,2,1:T(8,128)(2,1)S(1)}, u32[]{:S(2)}, u32[]{:S(2)}) collective-permute-start(bf16[12,3,2,2048]{3,0,2,1:T(8,128)(2,1)S(1)} %copy.98), channel_id=1, source_target_pairs={{0,1},{1,2},{2,3},{3,4},{4,5},{5,6},{6,7},{7,8},{8,9},{9,10},{10,1... | collective-permute-start | bytes 884744 | tf_op jit(solution)/shard_map/ppermute | solution.py:19
Sparse Core Ops, SparseCore 0:
  10.5 109.5 all-gather.2
  122.6 58.1 all-gather.4
  184.8 78.1 reduce-scatter.4
  267.8 133.1 reduce-scatter.2
where the time goes:
time: 418 us; the launch traced here: 411 us
  waiting for transfers between devices  116 us (28%)
  local copies, waits for them, and re-layouts  112 us (27%)
  matrix products  87.7 us (21%)
  blocking collectives  39.1 us (9%)
  starting transfers between devices  22.3 us (5%)
  other arithmetic  19.6 us (5%)
  between operations  14.3 us (3%)
    ppermute x6, waiting for transfers between devices, passed_along(): lax.ppermute(value, axis, [(i, (i + by) % devices) for i in range(devices)])  41.3 us
    unnamed x17, local copies, waits for them, and re-layouts  41.3 us
    all_to_all x1, blocking collectives, local(): lax.all_to_all(carried, 'lon', split_axis=3, concat_axis=1, tiled=True)  39.1 us
    all_gather x1, waiting for transfers between devices, local(): lax.all_gather(out_weight, 'lon', axis=0, tiled=True)  28 us
    all_gather x1, waiting for transfers between devices, local(): lax.all_gather(qkv_weight, 'lon', axis=0, tiled=True)  24.5 us
    convert_element_type x1, local copies, waits for them, and re-layouts, local(): (upstream.astype(jnp.float32) + carried.astype(jnp.float32)).astype(jnp.b...  23.7 us
    all_to_all x1, waiting for transfers between devices, local(): lax.all_to_all(tokens, 'lon', split_axis=1, concat_axis=3, tiled=True)  20.6 us
    all_to_all x1, local copies, waits for them, and re-layouts, local(): lax.all_to_all(carried, 'lon', split_axis=3, concat_axis=1, tiled=True)  19.9 us
  transfers between devices with their start and end apart: 11, of which 8 were waited for; matrix products, arithmetic and copies ran while one was open for 53% of the time, Pallas kernels for 0%

commit v1 on v0

v1 whole, which is shorter than its diff:
```python
import functools

import jax
import jax.numpy as jnp
from jax import lax
from jax.experimental import pallas as pl
from jax.experimental.pallas import tpu as pltpu
from jax.sharding import PartitionSpec as P

HEAD_DIM = 64
WLAT = 12
WLON = 6
LEVELS = 2
WTOK = WLAT * WLON * LEVELS
PAIR = 2 * WTOK
HALF = WTOK // 2
D = 2048
NY = 4
MIB = 1024 * 1024

NEG_FILL = -1e30
EPSILON = 1e-05


def lon_of(xh, y, c):
    return (xh * NY + y) * 2 + c


COORDS = [(xh, y, c) for xh in range(2) for y in range(NY) for c in range(2)]


ALONG_Y = [[lon_of(xh, y, c) for y in range(NY)] for xh in range(2) for c in range(2)]


def swap_c(value):
    return lax.ppermute(value, "lon", [(lon_of(x, y, c), lon_of(x, y, 1 - c)) for x, y, c in COORDS])


def swap_x(value):
    return lax.ppermute(value, "lon", [(lon_of(x, y, c), lon_of(1 - x, y, c)) for x, y, c in COORDS])


def shift_y(value, by):
    return lax.ppermute(value, "lon", [(lon_of(x, y, c), lon_of(x, (y + by) % NY, c)) for x, y, c in COORDS])


def moved(value, dlat, lon_map):
    rows, lons = lax.axis_size("lat"), lax.axis_size("lon")
    pairs = [
        (r * lons + i, (r + dlat) % rows * lons + lon_map(i)) for r in range(rows) for i in range(lons)
    ]
    return lax.ppermute(value, ("lat", "lon"), pairs)


def y_map(by):
    return lambda i: lon_of(i // 8, (i // 2 + by) % NY, i % 2)


def x_map(i):
    return lon_of(1 - i // 8, i // 2 % NY, i % 2)


def lon_map(by):
    return lambda i: (i + by) % 16


def mm(a, b, dims):
    return lax.dot_general(a, b, (dims, ((), ())), preferred_element_type=jnp.float32)


def shape(dims, dtype=jnp.bfloat16):
    return jax.ShapeDtypeStruct(dims, dtype)


def whole(*dims):
    return pl.BlockSpec(dims, lambda *_: (0,) * len(dims))


def weight_split_kernel(s_ref, q_ref, o_ref, w_ref, out_ref):
    group = s_ref[0] * 2 + s_ref[1]
    for xh in range(2):
        for c in range(2):
            slot = group ^ (xh * 2 + c)
            for part in range(3):
                for pair in range(2):
                    lo = (part * 8 + xh * 4 + pair * 2) * 128 + c * 64
                    w_ref[slot, part * 2 + pair] = jnp.concatenate(
                        [q_ref[:, lo:lo + 64], q_ref[:, lo + 128:lo + 192]], axis=1)
    for i in range(8):
        out_ref[i] = jnp.concatenate(
            [o_ref[:, i * 256:i * 256 + 128], o_ref[:, i * 256 + 128:i * 256 + 256]], axis=0)


def weight_split(scalars, qkv_weight, out_weight):
    return pl.pallas_call(
        weight_split_kernel,
        grid_spec=pltpu.PrefetchScalarGridSpec(
            num_scalar_prefetch=1,
            grid=(1,),
            in_specs=[whole(128, 3072), whole(64, D)],
            out_specs=[whole(4, 6, 128, 128), whole(8, 128, 128)],
        ),
        out_shape=[shape((4, 6, 128, 128)), shape((8, 128, 128))],
        cost_estimate=pl.CostEstimate(flops=0, bytes_accessed=2 * 10**6, transcendentals=0),
        name="weight_split",
    )(scalars, qkv_weight, out_weight)


def weight_join_kernel(s_ref, a_ref, b_ref, c_ref, out_ref):
    group = s_ref[0] * 2 + s_ref[1]

    def block(slot, index):
        return jnp.where(slot == 0, a_ref[index], jnp.where(
            slot == 1, b_ref[0, index].astype(jnp.float32), jnp.where(
                slot == 3, b_ref[1, index], c_ref[0, index]).astype(jnp.float32)))

    for xh in range(2):
        slots = [group ^ (xh * 2), group ^ (xh * 2 + 1)]
        for part in range(3):
            for pair in range(2):
                left, right = (block(slot, part * 2 + pair) for slot in slots)
                lo = (part * 8 + xh * 4 + pair * 2) * 128
                out_ref[:, lo:lo + 128] = jnp.concatenate([left[:, :64], right[:, :64]], axis=1)
                out_ref[:, lo + 128:lo + 256] = jnp.concatenate([left[:, 64:], right[:, 64:]], axis=1)


def weight_join(scalars, own, by_c, by_x):
    return pl.pallas_call(
        weight_join_kernel,
        grid_spec=pltpu.PrefetchScalarGridSpec(
            num_scalar_prefetch=1,
            grid=(1,),
            in_specs=[whole(6, 128, 128), whole(2, 6, 128, 128), whole(2, 6, 128, 128)],
            out_specs=whole(128, 3072),
        ),
        out_shape=shape((128, 3072), jnp.float32),
        cost_estimate=pl.CostEstimate(flops=0, bytes_accessed=3 * 10**6, transcendentals=0),
        name="weight_join",
    )(scalars, own, by_c, by_x)


def spans(y):
    for s in range(4):
        for w in range(2):
            for t in range(4):
                xh, c = t // 2, t % 2
                start = 12 * lon_of(xh, lax.rem(y + s, 4), c) + 3 + 6 * w
                if xh == 1 and c == 1 and w == 1:
                    yield s, w, t, start, 0, 3
                    yield s, w, t, lax.rem(start + 3, 192), 3, 3
                else:
                    yield s, w, t, start, 0, 6


def token_split_kernel(s_ref, tok_ref, *outs):
    for s, w, t, start, offset, columns in spans(s_ref[2]):
        for half in range(2):
            outs[s][half, w, t, :, offset:offset + columns] = (
                tok_ref[6 - half * 6:12 - half * 6, pl.ds(start, columns)])


def token_split(scalars, tokens):
    dims = (2, 2, 4, 6, WLON, LEVELS, 128)
    return pl.pallas_call(
        token_split_kernel,
        grid_spec=pltpu.PrefetchScalarGridSpec(
            num_scalar_prefetch=1,
            grid=(1,),
            in_specs=[whole(WLAT, 192, LEVELS, 128)],
            out_specs=[whole(*dims)] * 4,
        ),
        out_shape=[shape(dims)] * 4,
        compiler_params=pltpu.CompilerParams(vmem_limit_bytes=40 * MIB),
        cost_estimate=pl.CostEstimate(flops=0, bytes_accessed=3 * 10**6, transcendentals=0),
        name="token_split",
    )(scalars, tokens)


def token_join_kernel(s_ref, *refs):
    parts, out_ref = refs[:4], refs[4]
    for s, w, t, start, offset, columns in spans(s_ref[2]):
        out_ref[6:12, pl.ds(start, columns)] = parts[s][w, t, 0:6, offset:offset + columns]
        out_ref[0:6, pl.ds(start, columns)] = parts[s][w, t, 6:12, offset:offset + columns]


def token_join(scalars, parts):
    return pl.pallas_call(
        token_join_kernel,
        grid_spec=pltpu.PrefetchScalarGridSpec(
            num_scalar_prefetch=1,
            grid=(1,),
            in_specs=[whole(2, 4, WLAT, WLON, LEVELS, 128)] * 4,
            out_specs=whole(WLAT, 192, LEVELS, 128),
        ),
        out_shape=shape((WLAT, 192, LEVELS, 128)),
        compiler_params=pltpu.CompilerParams(vmem_limit_bytes=40 * MIB),
        cost_estimate=pl.CostEstimate(flops=0, bytes_accessed=3 * 10**6, transcendentals=0),
        name="token_join",
    )(scalars, *parts)


def attend(qkv, grad_att, split):
    scale = HEAD_DIM ** -0.5
    lane = lax.broadcasted_iota(jnp.int32, (1, 128), 1)
    row_group = lax.broadcasted_iota(jnp.int32, (WTOK, WTOK), 0) >= HALF
    col_group = lax.broadcasted_iota(jnp.int32, (WTOK, WTOK), 1) >= HALF
    keep = (row_group == col_group) | (split == 0)
    units = []
    for w in range(2):
        rows = slice(w * WTOK, (w + 1) * WTOK)
        for pair in range(2):
            cols = slice(pair * 128, (pair + 1) * 128)
            q = qkv[rows, 0:256][:, cols] * scale
            k = qkv[rows, 256:512][:, cols]
            v = qkv[rows, 512:768][:, cols]
            g = grad_att[rows, cols]
            heads = []
            for h in range(2):
                mine = (lane < 64) == (h == 0)
                heads.append((
                    jnp.where(mine, q, 0.0).astype(jnp.bfloat16),
                    jnp.where(mine, g, 0.0).astype(jnp.bfloat16),
                ))
            kb, vb = k.astype(jnp.bfloat16), v.astype(jnp.bfloat16)
            units.append((heads, kb, vb, k.T.astype(jnp.bfloat16), v.T.astype(jnp.bfloat16)))
    work = [(u, h) for u in range(4) for h in range(2)]
    scores = {
        (u, h): mm(units[u][1], units[u][0][h][0], ((1,), (1,))) for u, h in work
    }
    probs, probs_b = {}, {}
    for key in work:
        kept = jnp.where(keep, scores[key], NEG_FILL)
        expons = jnp.exp(kept - jnp.max(kept, axis=0, keepdims=True))
        probs[key] = expons * (1.0 / jnp.sum(expons, axis=0, keepdims=True))
        probs_b[key] = probs[key].astype(jnp.bfloat16)
    grads = {}
    for u, h in work:
        weighted = probs[u, h] * mm(units[u][2], units[u][0][h][1], ((1,), (1,)))
        inner = jnp.sum(weighted, axis=0, keepdims=True)
        grads[u, h] = (weighted - probs[u, h] * inner).astype(jnp.bfloat16)
    att, dq, dk, dv = [], [], [], []
    for u in range(4):
        heads, _, _, kt, vt = units[u]
        att.append(jnp.concatenate(
            [mm(vt[h * 64:(h + 1) * 64], probs_b[u, h], ((1,), (0,))) for h in range(2)], axis=0).T)
        dq.append(jnp.concatenate(
            [mm(kt[h * 64:(h + 1) * 64], grads[u, h], ((1,), (0,))) for h in range(2)], axis=0).T * scale)
        dk.append(sum(mm(grads[u, h], heads[h][0], ((1,), (0,))) for h in range(2)))
        dv.append(sum(mm(probs_b[u, h], heads[h][1], ((1,), (0,))) for h in range(2)))
    attended = jnp.concatenate([jnp.concatenate(att[2 * w:2 * w + 2], axis=1) for w in range(2)], axis=0)
    dqkv = jnp.concatenate([
        jnp.concatenate(dq[2 * w:2 * w + 2] + dk[2 * w:2 * w + 2] + dv[2 * w:2 * w + 2], axis=1)
        for w in range(2)], axis=0)
    return attended.astype(jnp.bfloat16), dqkv.astype(jnp.bfloat16)


def window_kernel(s_ref, *refs):
    xs, us, w_ref = refs[:4], refs[4:8], refs[8]
    pc_ref, px_ref, po_ref, term_ref = refs[9:13]
    wfull, wout, ub, gacc, nb_all, dq_all = refs[13:]
    i = pl.program_id(0)
    c, y = s_ref[1], s_ref[2]

    @pl.when(i == 0)
    def _():
        for s in range(4):
            head = lax.rem(y + 4 - s, 4)

            def block(index):
                return w_ref[head * 32 + index]

            for k in range(4):
                row = (s * 4 + k) * 128
                for part in range(6):
                    wfull[row:row + 128, part * 128:(part + 1) * 128] = block(k * 6 + part)
            rows = pl.ds(pl.multiple_of(head * 64, 64), 64)
            for j in range(8):
                wout[rows, j * 256:j * 256 + 128] = block(24 + j)[0:64]
                wout[rows, j * 256 + 128:j * 256 + 256] = block(24 + j)[64:128]
        gacc[...] = jnp.zeros_like(gacc)

    for step in range(4):
        @pl.when(i == step)
        def _():
            for dc in range(2):
                ub[pl.ds(pl.multiple_of((dc ^ c) * WTOK, WTOK), WTOK), :] = us[2 * (step % 2) + dc][0]

    x = jnp.concatenate(
        [xs[k][s, 0].reshape(PAIR, 128) for s in range(4) for k in range(4)], axis=1
    ).astype(jnp.float32)
    centred = x - jnp.mean(x, axis=-1, keepdims=True)
    inverse = lax.rsqrt(jnp.mean(centred * centred, axis=-1, keepdims=True) + EPSILON)
    nb = (centred * inverse).astype(jnp.bfloat16)
    rows = pl.ds(pl.multiple_of(i * PAIR, PAIR), PAIR)
    nb_all[rows, :] = nb
    qkv = mm(nb, wfull[...], ((1,), (0,)))
    grad_att = mm(ub[...], wout[...], ((1,), (1,)))
    attended, dqkv = attend(qkv, grad_att, s_ref[3])
    dq_all[rows, :] = dqkv
    gacc[...] += mm(attended, ub[...], ((0,), (0,)))
    grad_normal = mm(dqkv, wfull[...], ((1,), (1,)))
    normal = nb_all[rows, :].astype(jnp.float32)
    mean_one = jnp.mean(grad_normal, axis=-1, keepdims=True)
    mean_two = jnp.mean(grad_normal * normal, axis=-1, keepdims=True)
    grad_rolled = inverse * (grad_normal - mean_one - normal * mean_two)

    for s in range(4):
        part = [grad_rolled[:, (s * 4 + k) * 128:(s * 4 + k + 1) * 128].reshape(2, WTOK, 128) for k in range(4)]
        pc_ref[0, s, 0] = part[1].astype(jnp.bfloat16)
        pc_ref[1, s, 0] = part[3].astype(jnp.bfloat16)
        px_ref[s, 0] = part[2].astype(jnp.bfloat16)
        block = lon_of(s_ref[0], lax.rem(y + 4 - s, 4), c)
        own = ub[:, pl.ds(pl.multiple_of(block * 128, 128), 128)].astype(jnp.float32)
        po_ref[s, 0] = part[0] + own.reshape(2, WTOK, 128)

    @pl.when(i == 3)
    def _():
        for s in range(4):
            head = lax.rem(y + 4 - s, 4)
            term = mm(nb_all[:, s * 512:(s + 1) * 512], dq_all[...], ((0,), (0,))).astype(jnp.bfloat16)
            for k in range(4):
                for part in range(6):
                    term_ref[head * 32 + k * 6 + part] = term[k * 128:(k + 1) * 128, part * 128:(part + 1) * 128]
            gw = gacc[pl.ds(pl.multiple_of(head * 64, 64), 64), :].astype(jnp.bfloat16)
            for j in range(8):
                term_ref[head * 32 + 24 + j] = jnp.concatenate(
                    [gw[:, j * 256:j * 256 + 128], gw[:, j * 256 + 128:j * 256 + 256]], axis=0)


def once(*dims):
    return pl.BlockSpec(dims, lambda *_: (0,) * len(dims), pipeline_mode=pl.Buffered(1))


def window_pass(scalars, xs, us, weights):
    tile = pl.BlockSpec((4, 1, 2, WTOK, 128), lambda i, s: (0, i // 2, (i % 2) ^ s[0], 0, 0))
    part_specs = [
        pl.BlockSpec((2, 4, 1, 2, WTOK, 128), lambda i, s: (0, 0, i // 2, (i % 2) ^ s[0], 0, 0)), tile, tile,
    ]
    part_shapes = [
        shape((2, 4, 2, 4, WTOK, 128)), shape((4, 2, 4, WTOK, 128)), shape((4, 2, 4, WTOK, 128), jnp.float32),
    ]
    return pl.pallas_call(
        window_kernel,
        grid_spec=pltpu.PrefetchScalarGridSpec(
            num_scalar_prefetch=1,
            grid=(4,),
            in_specs=[tile] * 4 + [pl.BlockSpec((1, WTOK, D), lambda i, s: (i // 2, 0, 0))] * 4
            + [once(128, 128, 128)],
            out_specs=part_specs + [once(128, 128, 128)],
            scratch_shapes=[
                pltpu.VMEM((D, 768), jnp.bfloat16),
                pltpu.VMEM((256, D), jnp.bfloat16),
                pltpu.VMEM((PAIR, D), jnp.bfloat16),
                pltpu.VMEM((256, D), jnp.float32),
                pltpu.VMEM((4 * PAIR, D), jnp.bfloat16),
                pltpu.VMEM((4 * PAIR, 768), jnp.bfloat16),
            ],
        ),
        out_shape=part_shapes + [shape((128, 128, 128))],
        compiler_params=pltpu.CompilerParams(vmem_limit_bytes=60 * MIB),
        cost_estimate=pl.CostEstimate(flops=32 * 10**9, bytes_accessed=30 * 10**6, transcendentals=10**6),
        name="window_pass",
    )(scalars, *xs, *us, weights)


def after(values, *earlier):
    return lax.optimization_barrier(tuple(values) + earlier)[:len(values)]


def local(tokens, upstream, qkv_weight, out_weight):
    lon = lax.axis_index("lon")
    lat = lax.axis_index("lat")
    xh, y, c = lon // 8, (lon // 2) % 4, lon % 2
    last = (lat == lax.axis_size("lat") - 1).astype(jnp.int32)
    scalars = jnp.stack([jnp.int32(v) for v in (xh, c, y, last)])

    split, out_blocks = weight_split(scalars, qkv_weight, out_weight)
    from_c = swap_c(jnp.stack([split[1], split[3]]))
    from_x = swap_x(jnp.stack([split[2], from_c[1]]))

    stay = lon_map(0)
    next_cols = moved(upstream[:, :3], 0, lon_map(-1))
    cols = jnp.concatenate([upstream[:, 3:], next_cols], axis=1)
    cols = cols.reshape(2, 6, 2, WLON, LEVELS, D).transpose(0, 2, 1, 3, 4, 5)
    u_low, u_high = cols[0], cols[1]
    u_low, u_high = after((u_low, u_high), from_x)
    u_x = [swap_x(u_high), moved(u_low, -1, x_map)]
    u_own = [u_high, moved(u_low, -1, stay)]
    u_own, u_x = (jnp.concatenate(u, axis=1).reshape(2, WTOK, D) for u in (u_own, u_x))
    us = [u_own, swap_c(u_own), u_x, swap_c(u_x)]

    pieces = token_split(scalars, tokens)
    pieces = [pieces[0]] + [shift_y(pieces[s], s) for s in (1, 2, 3)]
    x_high = jnp.stack([piece[0] for piece in pieces])
    x_low = jnp.stack([piece[1] for piece in pieces])
    x_x = [swap_x(x_high), moved(x_low, -1, x_map)]
    x_own = [x_high, moved(x_low, -1, stay)]
    x_own, x_x = (jnp.concatenate(v, axis=3).reshape(4, 2, 4, WTOK, 128) for v in (x_own, x_x))

    shard = jnp.concatenate(
        [split[0], from_c[0], from_x.reshape(12, 128, 128), out_blocks])
    (shard,) = after((shard,), next_cols, *pieces[1:])
    weights = lax.all_gather(shard, "lon", axis=0, tiled=True, axis_index_groups=ALONG_Y)
    xs = [x_own, swap_c(x_own), x_x, swap_c(x_x)]

    part_c, part_x, part_own, terms = window_pass(scalars, xs, us, weights)

    got_c = swap_c(part_c)
    own = part_own + got_c[0].astype(jnp.float32)
    other = (part_x.astype(jnp.float32) + got_c[1].astype(jnp.float32)).astype(jnp.bfloat16)
    own_low = own[..., HALF:, :].astype(jnp.bfloat16)

    high = own[..., :HALF, :] + swap_x(other[..., :HALF, :]).astype(jnp.float32)
    low = moved(own_low, 1, stay).astype(jnp.float32) + moved(other[..., HALF:, :], 1, x_map).astype(jnp.float32)
    full = jnp.concatenate([high, low], axis=3).astype(jnp.bfloat16)
    back = [full[0]] + [shift_y(full[s], -s) for s in (1, 2, 3)]

    total = lax.psum_scatter(
        terms, "lon", scatter_dimension=0, tiled=True, axis_index_groups=ALONG_Y).astype(jnp.float32)
    (total,) = after((total,), full)
    blocks = total[:24].reshape(4, 6, 128, 128)
    sent = blocks.astype(jnp.bfloat16)
    by_x = swap_x(sent[2:])
    (near_x,) = after((by_x,), *back)
    by_c = swap_c(jnp.stack([sent[1], near_x[1]]))
    grad_qkv_w = weight_join(scalars, blocks[0], by_c, by_x)
    grad_out_w = total[24:].reshape(8, 2, 64, 128).transpose(2, 0, 1, 3).reshape(64, D)

    result = token_join(scalars, [b.reshape(2, 4, WLAT, WLON, LEVELS, 128) for b in back])
    return (result, grad_qkv_w[None], grad_out_w[None])


def solution(mesh):
    return jax.shard_map(
        local,
        mesh=mesh,
        in_specs=(
            P("lat", None, None, "lon"),
            P("lat", "lon", None, None),
            P("lon", None),
            P("lon", None),
        ),
        out_specs=(P("lat", None, None, "lon"), P("lat", "lon", None), P("lat", "lon", None)),
        check_vma=False,
    )
```

time: 418 us -> 238 us (0.57); the launches traced: 411 us -> 238 us
  local copies, waits for them, and re-layouts: 112 us -> 10.9 us
  matrix products: 87.7 us -> 0 us
  Pallas kernels: 0 us -> 43.4 us
  blocking collectives: 39.1 us -> 0 us
  starting transfers between devices: 22.3 us -> 36.8 us
    dot_general x10 -> x0, matrix products: 80.5 us -> none  [the longest x1 13.8 us: attention_backward(): jnp.einsum('hqk,khd->qhd', grad_scores, key_rows, preferred_element_type=...]
    ppermute x6 -> x25, waiting for transfers between devices: 41.3 us -> 112 us  [the longest x7 48.8 us: moved(): return lax.ppermute(value, ('lat', 'lon'), pairs)]
    all_gather x2 -> x1, waiting for transfers between devices: 52.5 us -> 0.01 us  [local(): lax.all_gather(shard, 'lon', axis=0, tiled=True, axis_index_groups=ALONG_Y)]
    pallas_call x0 -> x5, Pallas kernels: none -> 43.4 us  [the longest x1 34 us: window_pass(): pl.pallas_call(window_kernel, grid_spec=pltpu.PrefetchScalarGridSpec(num_...]
    unnamed x17 -> x24, local copies, waits for them, and re-layouts: 41.3 us -> 0.81 us
    all_to_all x1 -> x0, blocking collectives: 39.1 us -> none  [local(): lax.all_to_all(carried, 'lon', split_axis=3, concat_axis=1, tiled=True)]
    convert_element_type x3 -> x0, local copies, waits for them, and re-layouts: 29.2 us -> none  [the longest x1 23.7 us: local(): (upstream.astype(jnp.float32) + carried.astype(jnp.float32)).astype(jnp.b...]
    ppermute x6 -> x25, starting transfers between devices: 13.2 us -> 36.7 us  [the longest x5 14.7 us: swap_x(): lax.ppermute(value, 'lon', [(lon_of(x, y, c), lon_of(1 - x, y, c)) for x,...]
  transfers between devices with their start and end apart: 11 -> 27, of which waited for: 8 -> 16; matrix products, arithmetic and copies ran while one was open for 53% -> 9% of each run, Pallas kernels for 0% -> 1%
where the time goes in v1:
time: 238 us
  waiting for transfers between devices  117 us (49%)
  Pallas kernels  43.4 us (18%)
  starting transfers between devices  36.8 us (15%)
  other arithmetic  15.5 us (7%)
  between operations  14.4 us (6%)
  local copies, waits for them, and re-layouts  10.9 us (5%)
    ppermute x7, waiting for transfers between devices, moved(): return lax.ppermute(value, ('lat', 'lon'), pairs)  48.8 us
    pallas_call x1, Pallas kernels, window_pass(): pl.pallas_call(window_kernel, grid_spec=pltpu.PrefetchScalarGridSpec(num_...  34 us
    ppermute x5, waiting for transfers between devices, swap_x(): lax.ppermute(value, 'lon', [(lon_of(x, y, c), lon_of(1 - x, y, c)) for x,...  29.2 us
    ppermute x6, waiting for transfers between devices, shift_y(): lax.ppermute(value, 'lon', [(lon_of(x, y, c), lon_of(x, (y + by) % NY, c)...  23.8 us
    ppermute x5, starting transfers between devices, swap_x(): lax.ppermute(value, 'lon', [(lon_of(x, y, c), lon_of(1 - x, y, c)) for x,...  14.7 us
    ppermute x7, waiting for transfers between devices, swap_c(): lax.ppermute(value, 'lon', [(lon_of(x, y, c), lon_of(x, y, 1 - c)) for x,...  9.73 us
    ppermute x7, starting transfers between devices, swap_c(): lax.ppermute(value, 'lon', [(lon_of(x, y, c), lon_of(x, y, 1 - c)) for x,...  9.33 us
    ppermute x6, starting transfers between devices, shift_y(): lax.ppermute(value, 'lon', [(lon_of(x, y, c), lon_of(x, (y + by) % NY, c)...  7.79 us
  transfers between devices with their start and end apart: 27, of which 16 were waited for; matrix products, arithmetic and copies ran while one was open for 9% of the time, Pallas kernels for 1%

profile of v1, /device:TPU:1, one launch (start us, length us, event | category | flops | bytes accessed | tf_op | source)
XLA Modules:
  0.0 238.1 jit_solution(11293591633344300821)
XLA Ops:
  7.3 0.7 pad_add_fusion.s_ref
  7.9 3.1 %weight_split.1 = (bf16[4,6,128,128]{3,2,1,0:T(8,128)(2,1)}, bf16[8,128,128]{2,1,0:T(8,128)(2,1)}) custom-call(s32[4]{0:T(128)} %pad_add_fusion.s_ref, bf16[128,3072]{1,0:T(8,128)(2,1)} %q_ref.1, bf16[64,2048]{1,0:T(8,128)(2,1)} %o_ref.1), custom_call_target="tpu_custom_call" | custom-call | bytes 2000000 | tf_op jit(solution)/shard_map/weight_split/pallas_call | solution.py:95
  11.0 1.3 slice_bitcast_fusion.6
  12.3 1.5 collective-permute-start.9
  13.8 1.3 collective-permute-done.9
  15.3 2.9 %collective-permute-start.10 = (bf16[2,6,128,128]{3,2,1,0:T(8,128)(2,1)S(1)}, bf16[2,6,128,128]{3,2,1,0:T(8,128)(2,1)S(1)}, u32[]{:S(2)}, u32[]{:S(2)}) collective-permute-start(bf16[2,6,128,128]{3,2,1,0:T(8,128)(2,1)S(1)} %pad_maximum_fusion.10), channel_id=1, source_target_pairs={{0,8},{1,9},{2,10},{3,11},{4,12},{5,13},{6,14},{7,15},{8,0},{9,1},... | collective-permute-start | bytes 1179656 | tf_op jit(solution)/shard_map/ppermute | solution.py:40
  18.2 0.9 slice.121
  19.1 0.7 collective-permute-start.8
  19.8 0.9 token_split.1
  20.6 1.4 collective-permute-start
  22.0 2.6 %collective-permute-start.1 = (bf16[2,2,4,6,6,2,128]{6,5,4,3,2,1,0:T(2,128)(2,1)S(1)}, bf16[2,2,4,6,6,2,128]{6,5,4,3,2,1,0:T(2,128)(2,1)S(1)}, u32[]{:S(2)}, u32[]{:S(2)}) collective-permute-start(bf16[2,2,4,6,6,2,128]{6,5,4,3,2,1,0:T(2,128)(2,1)S(1)} %get-tuple-element.20), channel_id=1, source_target_pairs={{0,4},{1,5},{2,6},{3,7},{4,0},{5,1},{6,2},{7,3},{8,12},{9,13},{10,... | collective-permute-start | bytes 884744 | tf_op jit(solution)/shard_map/ppermute | solution.py:44
  24.6 1.1 collective-permute-start.2
  25.7 1.5 collective-permute-done.10
  27.2 1.1 pad_maximum_fusion.6
  28.3 9.6 %collective-permute-done.1 = bf16[2,2,4,6,6,2,128]{6,5,4,3,2,1,0:T(2,128)(2,1)S(1)} collective-permute-done((bf16[2,2,4,6,6,2,128]{6,5,4,3,2,1,0:T(2,128)(2,1)S(1)}, bf16[2,2,4,6,6,2,128]{6,5,4,3,2,1,0:T(2,128)(2,1)S(1)}, u32[]{:S(2)}, u32[]{:S(2)}) %collective-permute-start.1) | collective-permute-done | bytes 294944 | tf_op jit(solution)/shard_map/ppermute | solution.py:44
  37.9 2.6 %collective-permute-done.2 = bf16[2,2,4,6,6,2,128]{6,5,4,3,2,1,0:T(2,128)(2,1)S(1)} collective-permute-done((bf16[2,2,4,6,6,2,128]{6,5,4,3,2,1,0:T(2,128)(2,1)S(1)}, bf16[2,2,4,6,6,2,128]{6,5,4,3,2,1,0:T(2,128)(2,1)S(1)}, u32[]{:S(2)}, u32[]{:S(2)}) %collective-permute-start.2) | collective-permute-done | bytes 294944 | tf_op jit(solution)/shard_map/ppermute | solution.py:44
  40.6 0.2 fusion.10
  40.8 0.2 fusion.11
  41.0 0.2 fusion.12
  41.3 0.2 fusion.13
  41.5 1.1 pad_maximum_fusion.8
  42.6 3.8 %collective-permute-start.6 = (bf16[4,2,4,6,6,2,128]{6,5,4,3,2,1,0:T(2,128)(2,1)S(1)}, bf16[4,2,4,6,6,2,128]{6,5,4,3,2,1,0:T(2,128)(2,1)S(1)}, u32[]{:S(2)}, u32[]{:S(2)}) collective-permute-start(bf16[4,2,4,6,6,2,128]{6,5,4,3,2,1,0:T(2,128)(2,1)S(1)} %pad_maximum_fusion.8), channel_id=1, source_target_pairs={{0,120},{1,121},{2,122},{3,123},{4,124},{5,125},{6,126},{7,127},{8... | collective-permute-start | bytes 1769480 | tf_op jit(solution)/shard_map/ppermute | solution.py:52
  46.3 0.2 collective-permute-start.3
  46.5 1.5 pad_maximum_fusion.3
  48.0 1.1 pad_maximum_fusion.7
  49.1 1.0 copy.12
  50.1 3.5 %collective-permute-start.5 = (bf16[4,2,4,6,6,2,128]{6,5,4,3,2,1,0:T(2,128)(2,1)S(1)}, bf16[4,2,4,6,6,2,128]{6,5,4,3,2,1,0:T(2,128)(2,1)S(1)}, u32[]{:S(2)}, u32[]{:S(2)}) collective-permute-start(bf16[4,2,4,6,6,2,128]{6,5,4,3,2,1,0:T(2,128)(2,1)S(1)} %pad_maximum_fusion.7), channel_id=1, source_target_pairs={{0,8},{1,9},{2,10},{3,11},{4,12},{5,13},{6,14},{7,15},{8,0},{9,1},... | collective-permute-start | bytes 1769480 | tf_op jit(solution)/shard_map/ppermute | solution.py:40
  53.6 0.8 slice_bitcast_fusion.2
  54.6 11.8 %collective-permute-done.3 = bf16[4,2,4,6,6,2,128]{6,5,4,3,2,1,0:T(2,128)(2,1)S(1)} collective-permute-done((bf16[4,2,4,6,6,2,128]{6,5,4,3,2,1,0:T(2,128)(2,1)S(1)}, bf16[4,2,4,6,6,2,128]{6,5,4,3,2,1,0:T(2,128)(2,1)S(1)}, u32[]{:S(2)}, u32[]{:S(2)}) %collective-permute-start.3) | collective-permute-done | bytes 589856 | tf_op jit(solution)/shard_map/ppermute | solution.py:52
  66.4 4.7 %collective-permute-start.13 = (bf16[2,6,6,2,2048]{4,3,2,1,0:T(2,128)(2,1)S(1)}, bf16[2,6,6,2,2048]{4,3,2,1,0:T(2,128)(2,1)S(1)}, u32[]{:S(2)}, u32[]{:S(2)}) collective-permute-start(bf16[2,6,6,2,2048]{4,3,2,1,0:T(2,128)(2,1)S(1)} %get-tuple-element.23), channel_id=1, source_target_pairs={{0,8},{1,9},{2,10},{3,11},{4,12},{5,13},{6,14},{7,15},{8,0},{9,1},... | collective-permute-start | bytes 1769480 | tf_op jit(solution)/shard_map/ppermute | solution.py:40
  71.1 1.9 pad_maximum_fusion.1
  73.0 11.4 %collective-permute-done.5 = bf16[4,2,4,6,6,2,128]{6,5,4,3,2,1,0:T(2,128)(2,1)S(1)} collective-permute-done((bf16[4,2,4,6,6,2,128]{6,5,4,3,2,1,0:T(2,128)(2,1)S(1)}, bf16[4,2,4,6,6,2,128]{6,5,4,3,2,1,0:T(2,128)(2,1)S(1)}, u32[]{:S(2)}, u32[]{:S(2)}) %collective-permute-start.5) | collective-permute-done | bytes 589856 | tf_op jit(solution)/shard_map/ppermute | solution.py:40
  84.5 2.7 %collective-permute-start.4 = (bf16[4,2,4,144,128]{4,3,2,1,0:T(8,128)(2,1)S(1)}, bf16[4,2,4,144,128]{4,3,2,1,0:T(8,128)(2,1)}, u32[]{:S(2)}, u32[]{:S(2)}) collective-permute-start(bf16[4,2,4,144,128]{4,3,2,1,0:T(8,128)(2,1)S(1)} %bitcast.54), channel_id=1, source_target_pairs={{0,1},{1,0},{2,3},{3,2},{4,5},{5,4},{6,7},{7,6},{8,9},{9,8},{10,11... | collective-permute-start | bytes 3538952 | tf_op jit(solution)/shard_map/ppermute | solution.py:36
  87.2 2.5 %pad_maximum_fusion.2 = bf16[4,2,4,12,6,2,128]{6,5,4,3,2,1,0:T(2,128)(2,1)} fusion(bf16[4,2,4,6,6,2,128]{6,5,4,3,2,1,0:T(2,128)(2,1)S(1)} %collective-permute-done.6, bf16[4,2,4,6,6,2,128]{6,5,4,3,2,1,0:T(2,128)(2,1)S(1)} %collective-permute-done.5), kind=kLoop, calls=%fused_computation.18 | loop fusion | flops 589824 | bytes 2359296 | tf_op jit(solution)/shard_map/concatenate | solution.py:398
  89.7 5.6 %collective-permute-done.11 = bf16[2,6,6,2,2048]{4,3,2,1,0:T(2,128)(2,1)S(1)} collective-permute-done((bf16[2,6,6,2,2048]{4,3,2,1,0:T(2,128)(2,1)S(1)}, bf16[2,6,6,2,2048]{4,3,2,1,0:T(2,128)(2,1)S(1)}, u32[]{:S(2)}, u32[]{:S(2)}) %collective-permute-start.11) | collective-permute-done | bytes 589856 | tf_op jit(solution)/shard_map/ppermute | solution.py:52
  95.3 1.5 pad_maximum_fusion.4
  96.8 16.3 %collective-permute-done.13 = bf16[2,6,6,2,2048]{4,3,2,1,0:T(2,128)(2,1)S(1)} collective-permute-done((bf16[2,6,6,2,2048]{4,3,2,1,0:T(2,128)(2,1)S(1)}, bf16[2,6,6,2,2048]{4,3,2,1,0:T(2,128)(2,1)S(1)}, u32[]{:S(2)}, u32[]{:S(2)}) %collective-permute-start.13) | collective-permute-done | bytes 589856 | tf_op jit(solution)/shard_map/ppermute | solution.py:40
  113.1 1.5 pad_maximum_fusion.5
  114.7 1.3 reshape.50.refs_6_
  116.0 1.3 reshape.49.refs_4_
  117.2 1.6 collective-permute-start.12
  118.8 0.3 collective-permute-start.15
  119.1 2.4 %collective-permute-done.12.refs_5_ = bf16[2,144,2048]{2,1,0:T(8,128)(2,1)S(1)} collective-permute-done((bf16[2,144,2048]{2,1,0:T(8,128)(2,1)}, bf16[2,144,2048]{2,1,0:T(8,128)(2,1)S(1)}, u32[]{:S(2)}, u32[]{:S(2)}) %collective-permute-start.12) | collective-permute-done | bytes 1179680 | tf_op jit(solution)/shard_map/ppermute | solution.py:36
  121.5 1.6 collective-permute-done.15.refs_7_
  123.1 34.0 %window_pass.1 = (bf16[2,4,2,4,144,128]{5,4,3,2,1,0:T(8,128)(2,1)}, bf16[4,2,4,144,128]{4,3,2,1,0:T(8,128)(2,1)}, f32[4,2,4,144,128]{4,3,2,1,0:T(8,128)}, bf16[128,128,128]{2,1,0:T(8,128)(2,1)}) custom-call(s32[4]{0:T(128)} %pad_add_fusion.s_ref, bf16[4,2,4,144,128]{4,3,2,1,0:T(8,128)(2,1)} %bitcast.55, ...), custom_call_target="tpu_custom_call" | custom-call | flops 32000000000 | bytes 30000000 | tf_op jit(solution)/shard_map/window_pass/pallas_call | solution.py:342
  157.2 0.5 collective-permute-start.16
  157.6 4.4 %collective-permute-done.16 = bf16[2,4,2,4,144,128]{5,4,3,2,1,0:T(8,128)(2,1)S(1)} collective-permute-done((bf16[2,4,2,4,144,128]{5,4,3,2,1,0:T(8,128)(2,1)}, bf16[2,4,2,4,144,128]{5,4,3,2,1,0:T(8,128)(2,1)S(1)}, u32[]{:S(2)}, u32[]{:S(2)}) %collective-permute-start.16) | collective-permute-done | bytes 2359328 | tf_op jit(solution)/shard_map/ppermute | solution.py:36
  162.0 0.5 fusion
  162.9 0.8 collective-permute-start.17
  163.7 20.7 %collective-permute-done.18 = bf16[4,2,4,72,128]{4,3,2,1,0:T(8,128)(2,1)S(1)} collective-permute-done((bf16[4,2,4,72,128]{4,3,2,1,0:T(8,128)(2,1)S(1)}, bf16[4,2,4,72,128]{4,3,2,1,0:T(8,128)(2,1)S(1)}, u32[]{:S(2)}, u32[]{:S(2)}) %collective-permute-start.18) | collective-permute-done | bytes 589856 | tf_op jit(solution)/shard_map/ppermute | solution.py:52
  184.4 10.7 %collective-permute-done.19 = bf16[4,2,4,72,128]{4,3,2,1,0:T(8,128)(2,1)S(1)} collective-permute-done((bf16[4,2,4,72,128]{4,3,2,1,0:T(8,128)(2,1)S(1)}, bf16[4,2,4,72,128]{4,3,2,1,0:T(8,128)(2,1)S(1)}, u32[]{:S(2)}, u32[]{:S(2)}) %collective-permute-start.19) | collective-permute-done | bytes 589856 | tf_op jit(solution)/shard_map/ppermute | solution.py:52
  195.4 5.5 %reduce-scatter.2.cloned.1.call-done = bf16[32,128,128]{2,1,0:T(8,128)(2,1)} async-done(((bf16[128,128,128]{2,1,0:T(8,128)(2,1)}), bf16[32,128,128]{2,1,0:T(8,128)(2,1)}) %reduce-scatter.2.cloned.1.call-update) | async-done | bytes 1048592 | tf_op jit(solution)/shard_map/reduce_scatter | solution.py:418
  200.9 1.5 convert_element_type.44
  202.5 2.8 %collective-permute-start.23 = (bf16[2,6,128,128]{3,2,1,0:T(8,128)(2,1)S(1)}, bf16[2,6,128,128]{3,2,1,0:T(8,128)(2,1)S(1)}, u32[]{:S(2)}, u32[]{:S(2)}) collective-permute-start(bf16[2,6,128,128]{3,2,1,0:T(8,128)(2,1)S(1)} %bitcast.57), channel_id=1, source_target_pairs={{0,8},{1,9},{2,10},{3,11},{4,12},{5,13},{6,14},{7,15},{8,0},{9,1},... | collective-permute-start | bytes 1179656 | tf_op jit(solution)/shard_map/ppermute | solution.py:40
  205.5 2.7 %collective-permute-start.20 = (bf16[2,4,144,128]{3,2,1,0:T(8,128)(2,1)S(1)}, bf16[2,4,144,128]{3,2,1,0:T(8,128)(2,1)S(1)}, u32[]{:S(2)}, u32[]{:S(2)}) collective-permute-start(bf16[2,4,144,128]{3,2,1,0:T(8,128)(2,1)S(1)} %get-tuple-element.36), channel_id=1, source_target_pairs={{0,6},{1,7},{2,0},{3,1},{4,2},{5,3},{6,4},{7,5},{8,14},{9,15},{10,... | collective-permute-start | bytes 884744 | tf_op jit(solution)/shard_map/ppermute | solution.py:44
  208.2 7.1 %collective-permute-done.22 = bf16[2,4,144,128]{3,2,1,0:T(8,128)(2,1)S(1)} collective-permute-done((bf16[2,4,144,128]{3,2,1,0:T(8,128)(2,1)S(1)}, bf16[2,4,144,128]{3,2,1,0:T(8,128)(2,1)S(1)}, u32[]{:S(2)}, u32[]{:S(2)}) %collective-permute-start.22) | collective-permute-done | bytes 294944 | tf_op jit(solution)/shard_map/ppermute | solution.py:44
  215.3 4.4 %collective-permute-done.21 = bf16[2,4,144,128]{3,2,1,0:T(8,128)(2,1)S(1)} collective-permute-done((bf16[2,4,144,128]{3,2,1,0:T(8,128)(2,1)S(1)}, bf16[2,4,144,128]{3,2,1,0:T(8,128)(2,1)S(1)}, u32[]{:S(2)}, u32[]{:S(2)}) %collective-permute-start.21) | collective-permute-done | bytes 294944 | tf_op jit(solution)/shard_map/ppermute | solution.py:44
  219.8 2.8 %collective-permute-start.24 = (bf16[2,6,128,128]{3,2,1,0:T(8,128)(2,1)S(1)}, bf16[2,6,128,128]{3,2,1,0:T(8,128)(2,1)S(1)}, u32[]{:S(2)}, u32[]{:S(2)}) collective-permute-start(bf16[2,6,128,128]{3,2,1,0:T(8,128)(2,1)S(1)} %pad_maximum_fusion.11), channel_id=1, source_target_pairs={{0,1},{1,0},{2,3},{3,2},{4,5},{5,4},{6,7},{7,6},{8,9},{9,8},{10,11... | collective-permute-start | bytes 1179656 | tf_op jit(solution)/shard_map/ppermute | solution.py:36
  222.6 1.9 token_join.1
  224.5 0.8 slice.140.a_ref
  225.3 0.4 copy.10
  225.7 1.2 broadcast_in_dim_reshape.3
  227.0 0.8 copy-done.9
  227.7 3.5 %weight_join.1 = f32[128,3072]{1,0:T(8,128)} custom-call(s32[4]{0:T(128)} %pad_add_fusion.s_ref, f32[6,128,128]{2,1,0:T(8,128)} %slice.140.a_ref, bf16[2,6,128,128]{3,2,1,0:T(8,128)(2,1)} %copy-done.9, bf16[2,6,128,128]{3,2,1,0:T(8,128)(2,1)} %copy-done.8), custom_call_target="tpu_custom_call" | custom-call | bytes 3000000 | tf_op jit(solution)/shard_map/weight_join/pallas_call | solution.py:128
  (61 shorter events, 1.6 us)
Async XLA Ops:
  7.2 115.9 %all-gather.2.cloned.1.call-start = ((), (), s32[]{:S(2)}) async-start(), calls=%async_computation.1 | async-start | bytes 5242880 | tf_op jit(solution)/shard_map/all_gather | solution.py:403
  12.3 5.9 %copy-start.3 = (bf16[12,12,2,2048]{3,2,1,0:T(2,128)(2,1)S(1)}, bf16[12,12,2,2048]{3,2,1,0:T(2,128)(2,1)}, u32[]{:S(2)}) copy-start(bf16[12,12,2,2048]{3,2,1,0:T(2,128)(2,1)} %param.5) | copy-start | bytes 3538948
  12.3 7.4 %copy-start = (bf16[12,192,2,128]{3,2,1,0:T(2,128)(2,1)S(1)}, bf16[12,192,2,128]{3,2,1,0:T(2,128)(2,1)}, u32[]{:S(2)}) copy-start(bf16[12,192,2,128]{3,2,1,0:T(2,128)(2,1)} %tok_ref.1) | copy-start | bytes 3538948
  12.3 7.4 %copy-start.1 = (s32[4]{0:T(128)S(1)}, s32[4]{0:T(128)}, u32[]{:S(2)}) copy-start(s32[4]{0:T(128)} %pad_add_fusion.s_ref) | copy-start | bytes 52
  12.3 2.9 %collective-permute-start.9 = (bf16[2,6,128,128]{3,2,1,0:T(8,128)(2,1)S(1)}, bf16[2,6,128,128]{3,2,1,0:T(8,128)(2,1)S(1)}, u32[]{:S(2)}, u32[]{:S(2)}) collective-permute-start(bf16[2,6,128,128]{3,2,1,0:T(8,128)(2,1)S(1)} %pad_maximum_fusion.9), channel_id=1, source_target_pairs={{0,1},{1,0},{2,3},{3,2},{4,5},{5,4},{6,7},{7,6},{8,9},{9,8},{10,11... | collective-permute-start | bytes 1179656 | tf_op jit(solution)/shard_map/ppermute | solution.py:36
  15.2 12.0 %copy-start.10 = (bf16[8,128,128]{2,1,0:T(8,128)(2,1)S(1)}, bf16[8,128,128]{2,1,0:T(8,128)(2,1)}, u32[]{:S(2)}) copy-start(bf16[8,128,128]{2,1,0:T(8,128)(2,1)} %get-tuple-element.25) | copy-start | bytes 786436
  15.3 11.9 %collective-permute-start.10 = (bf16[2,6,128,128]{3,2,1,0:T(8,128)(2,1)S(1)}, bf16[2,6,128,128]{3,2,1,0:T(8,128)(2,1)S(1)}, u32[]{:S(2)}, u32[]{:S(2)}) collective-permute-start(bf16[2,6,128,128]{3,2,1,0:T(8,128)(2,1)S(1)} %pad_maximum_fusion.10), channel_id=1, source_target_pairs={{0,8},{1,9},{2,10},{3,11},{4,12},{5,13},{6,14},{7,15},{8,0},{9,1},... | collective-permute-start | bytes 1179656 | tf_op jit(solution)/shard_map/ppermute | solution.py:40
  19.1 9.2 %collective-permute-start.8 = (bf16[12,3,2,2048]{3,2,1,0:T(2,128)(2,1)}, bf16[12,3,2,2048]{3,2,1,0:T(2,128)(2,1)S(1)}, u32[]{:S(2)}, u32[]{:S(2)}) collective-permute-start(bf16[12,3,2,2048]{3,2,1,0:T(2,128)(2,1)} %slice.121), channel_id=1, source_target_pairs={{0,15},{1,0},{2,1},{3,2},{4,3},{5,4},{6,5},{7,6},{8,7},{9,8},{10,9... | collective-permute-start | bytes 884744 | tf_op jit(solution)/shard_map/ppermute | solution.py:52
  20.6 7.7 %collective-permute-start = (bf16[2,2,4,6,6,2,128]{6,5,4,3,2,1,0:T(2,128)(2,1)S(1)}, bf16[2,2,4,6,6,2,128]{6,5,4,3,2,1,0:T(2,128)(2,1)S(1)}, u32[]{:S(2)}, u32[]{:S(2)}) collective-permute-start(bf16[2,2,4,6,6,2,128]{6,5,4,3,2,1,0:T(2,128)(2,1)S(1)} %get-tuple-element.19), channel_id=1, source_target_pairs={{0,2},{1,3},{2,4},{3,5},{4,6},{5,7},{6,0},{7,1},{8,10},{9,11},{10,... | collective-permute-start | bytes 884744 | tf_op jit(solution)/shard_map/ppermute | solution.py:44
  22.0 15.9 %collective-permute-start.1 = (bf16[2,2,4,6,6,2,128]{6,5,4,3,2,1,0:T(2,128)(2,1)S(1)}, bf16[2,2,4,6,6,2,128]{6,5,4,3,2,1,0:T(2,128)(2,1)S(1)}, u32[]{:S(2)}, u32[]{:S(2)}) collective-permute-start(bf16[2,2,4,6,6,2,128]{6,5,4,3,2,1,0:T(2,128)(2,1)S(1)} %get-tuple-element.20), channel_id=1, source_target_pairs={{0,4},{1,5},{2,6},{3,7},{4,0},{5,1},{6,2},{7,3},{8,12},{9,13},{10,... | collective-permute-start | bytes 884744 | tf_op jit(solution)/shard_map/ppermute | solution.py:44
  24.6 15.9 %collective-permute-start.2 = (bf16[2,2,4,6,6,2,128]{6,5,4,3,2,1,0:T(2,128)(2,1)S(1)}, bf16[2,2,4,6,6,2,128]{6,5,4,3,2,1,0:T(2,128)(2,1)S(1)}, u32[]{:S(2)}, u32[]{:S(2)}) collective-permute-start(bf16[2,2,4,6,6,2,128]{6,5,4,3,2,1,0:T(2,128)(2,1)S(1)} %get-tuple-element.21), channel_id=1, source_target_pairs={{0,6},{1,7},{2,0},{3,1},{4,2},{5,3},{6,4},{7,5},{8,14},{9,15},{10,... | collective-permute-start | bytes 884744 | tf_op jit(solution)/shard_map/ppermute | solution.py:44
  40.6 160.3 %reduce-scatter.2.cloned.1.call-start = ((), (), s32[]{:S(2)}) async-start(), calls=%async_computation.2 | async-start | bytes 5242880 | tf_op jit(solution)/shard_map/reduce_scatter | solution.py:418
  41.0 5.5 %slice-start = ((bf16[12,12,2,2048]{3,2,1,0:T(2,128)(2,1)}), bf16[12,9,2,2048]{3,2,1,0:T(2,128)(2,1)S(1)}, s32[]{:S(2)}) async-start(bf16[12,12,2,2048]{3,2,1,0:T(2,128)(2,1)} %param.5), calls=%async_computation.3 | async-start | bytes 1769472 | tf_op jit(solution)/shard_map/slice | solution.py:383
  42.6 44.6 %collective-permute-start.6 = (bf16[4,2,4,6,6,2,128]{6,5,4,3,2,1,0:T(2,128)(2,1)S(1)}, bf16[4,2,4,6,6,2,128]{6,5,4,3,2,1,0:T(2,128)(2,1)S(1)}, u32[]{:S(2)}, u32[]{:S(2)}) collective-permute-start(bf16[4,2,4,6,6,2,128]{6,5,4,3,2,1,0:T(2,128)(2,1)S(1)} %pad_maximum_fusion.8), channel_id=1, source_target_pairs={{0,120},{1,121},{2,122},{3,123},{4,124},{5,125},{6,126},{7,127},{8... | collective-permute-start | bytes 1769480 | tf_op jit(solution)/shard_map/ppermute | solution.py:52
  46.3 20.1 %collective-permute-start.3 = (bf16[4,2,4,6,6,2,128]{6,5,4,3,2,1,0:T(2,128)(2,1)S(1)}, bf16[4,2,4,6,6,2,128]{6,5,4,3,2,1,0:T(2,128)(2,1)S(1)}, u32[]{:S(2)}, u32[]{:S(2)}) collective-permute-start(bf16[4,2,4,6,6,2,128]{6,5,4,3,2,1,0:T(2,128)(2,1)S(1)} %pad_maximum_fusion.8), channel_id=1, source_target_pairs={{0,112},{1,113},{2,114},{3,115},{4,116},{5,117},{6,118},{7,119},{8... | collective-permute-start | bytes 1769480 | tf_op jit(solution)/shard_map/ppermute | solution.py:52
  50.1 34.4 %collective-permute-start.5 = (bf16[4,2,4,6,6,2,128]{6,5,4,3,2,1,0:T(2,128)(2,1)S(1)}, bf16[4,2,4,6,6,2,128]{6,5,4,3,2,1,0:T(2,128)(2,1)S(1)}, u32[]{:S(2)}, u32[]{:S(2)}) collective-permute-start(bf16[4,2,4,6,6,2,128]{6,5,4,3,2,1,0:T(2,128)(2,1)S(1)} %pad_maximum_fusion.7), channel_id=1, source_target_pairs={{0,8},{1,9},{2,10},{3,11},{4,12},{5,13},{6,14},{7,15},{8,0},{9,1},... | collective-permute-start | bytes 1769480 | tf_op jit(solution)/shard_map/ppermute | solution.py:40
  54.5 58.7 %collective-permute-start.14 = (bf16[2,6,6,2,2048]{4,3,2,1,0:T(2,128)(2,1)S(1)}, bf16[2,6,6,2,2048]{4,3,2,1,0:T(2,128)(2,1)S(1)}, u32[]{:S(2)}, u32[]{:S(2)}) collective-permute-start(bf16[2,6,6,2,2048]{4,3,2,1,0:T(2,128)(2,1)S(1)} %get-tuple-element.24), channel_id=1, source_target_pairs={{0,120},{1,121},{2,122},{3,123},{4,124},{5,125},{6,126},{7,127},{8... | collective-permute-start | bytes 1769480 | tf_op jit(solution)/shard_map/ppermute | solution.py:52
  54.6 40.7 %collective-permute-start.11 = (bf16[2,6,6,2,2048]{4,3,2,1,0:T(2,128)(2,1)S(1)}, bf16[2,6,6,2,2048]{4,3,2,1,0:T(2,128)(2,1)S(1)}, u32[]{:S(2)}, u32[]{:S(2)}) collective-permute-start(bf16[2,6,6,2,2048]{4,3,2,1,0:T(2,128)(2,1)S(1)} %get-tuple-element.24), channel_id=1, source_target_pairs={{0,112},{1,113},{2,114},{3,115},{4,116},{5,117},{6,118},{7,119},{8... | collective-permute-start | bytes 1769480 | tf_op jit(solution)/shard_map/ppermute | solution.py:52
  66.4 46.7 %collective-permute-start.13 = (bf16[2,6,6,2,2048]{4,3,2,1,0:T(2,128)(2,1)S(1)}, bf16[2,6,6,2,2048]{4,3,2,1,0:T(2,128)(2,1)S(1)}, u32[]{:S(2)}, u32[]{:S(2)}) collective-permute-start(bf16[2,6,6,2,2048]{4,3,2,1,0:T(2,128)(2,1)S(1)} %get-tuple-element.23), channel_id=1, source_target_pairs={{0,8},{1,9},{2,10},{3,11},{4,12},{5,13},{6,14},{7,15},{8,0},{9,1},... | collective-permute-start | bytes 1769480 | tf_op jit(solution)/shard_map/ppermute | solution.py:40
  73.0 16.7 %copy-start.6 = (bf16[4,2,4,12,6,2,128]{6,5,4,3,2,1,0:T(2,128)(2,1)}, bf16[4,2,4,12,6,2,128]{6,5,4,3,2,1,0:T(2,128)(2,1)S(1)}, u32[]{:S(2)}) copy-start(bf16[4,2,4,12,6,2,128]{6,5,4,3,2,1,0:T(2,128)(2,1)S(1)} %pad_maximum_fusion.1) | copy-start | bytes 3538948
  84.5 34.6 %collective-permute-start.4 = (bf16[4,2,4,144,128]{4,3,2,1,0:T(8,128)(2,1)S(1)}, bf16[4,2,4,144,128]{4,3,2,1,0:T(8,128)(2,1)}, u32[]{:S(2)}, u32[]{:S(2)}) collective-permute-start(bf16[4,2,4,144,128]{4,3,2,1,0:T(8,128)(2,1)S(1)} %bitcast.54), channel_id=1, source_target_pairs={{0,1},{1,0},{2,3},{3,2},{4,5},{5,4},{6,7},{7,6},{8,9},{9,8},{10,11... | collective-permute-start | bytes 3538952 | tf_op jit(solution)/shard_map/ppermute | solution.py:36
  89.7 29.4 %collective-permute-start.7 = (bf16[4,2,4,144,128]{4,3,2,1,0:T(8,128)(2,1)}, bf16[4,2,4,144,128]{4,3,2,1,0:T(8,128)(2,1)}, u32[]{:S(2)}, u32[]{:S(2)}) collective-permute-start(bf16[4,2,4,144,128]{4,3,2,1,0:T(8,128)(2,1)} %bitcast.5.refs_2_), channel_id=1, source_target_pairs={{0,1},{1,0},{2,3},{3,2},{4,5},{5,4},{6,7},{7,6},{8,9},{9,8},{10,11... | collective-permute-start | bytes 3538952 | tf_op jit(solution)/shard_map/ppermute | solution.py:36
  116.0 2.8 %copy-start.7 = (bf16[2,144,2048]{2,1,0:T(8,128)(2,1)S(1)}, bf16[2,144,2048]{2,1,0:T(8,128)(2,1)}, u32[]{:S(2)}) copy-start(bf16[2,144,2048]{2,1,0:T(8,128)(2,1)} %reshape.50.refs_6_) | copy-start | bytes 3538948
  117.2 4.2 %collective-permute-start.12 = (bf16[2,144,2048]{2,1,0:T(8,128)(2,1)}, bf16[2,144,2048]{2,1,0:T(8,128)(2,1)S(1)}, u32[]{:S(2)}, u32[]{:S(2)}) collective-permute-start(bf16[2,144,2048]{2,1,0:T(8,128)(2,1)} %reshape.49.refs_4_), channel_id=1, source_target_pairs={{0,1},{1,0},{2,3},{3,2},{4,5},{5,4},{6,7},{7,6},{8,9},{9,8},{10,11... | collective-permute-start | bytes 3538952 | tf_op jit(solution)/shard_map/ppermute | solution.py:36
  118.8 4.3 %collective-permute-start.15 = (bf16[2,144,2048]{2,1,0:T(8,128)(2,1)S(1)}, bf16[2,144,2048]{2,1,0:T(8,128)(2,1)}, u32[]{:S(2)}, u32[]{:S(2)}) collective-permute-start(bf16[2,144,2048]{2,1,0:T(8,128)(2,1)S(1)} %copy-done.7), channel_id=1, source_target_pairs={{0,1},{1,0},{2,3},{3,2},{4,5},{5,4},{6,7},{7,6},{8,9},{9,8},{10,11... | collective-permute-start | bytes 3538952 | tf_op jit(solution)/shard_map/ppermute | solution.py:36
  121.5 1.6 copy-start.11
  157.1 4.9 %copy-start.4 = (f32[4,2,4,144,128]{4,3,2,1,0:T(8,128)S(1)}, f32[4,2,4,144,128]{4,3,2,1,0:T(8,128)}, u32[]{:S(2)}) copy-start(f32[4,2,4,144,128]{4,3,2,1,0:T(8,128)} %get-tuple-element.27) | copy-start | bytes 7077892
  157.1 4.9 %copy-start.5 = (bf16[4,2,4,144,128]{4,3,2,1,0:T(8,128)(2,1)S(1)}, bf16[4,2,4,144,128]{4,3,2,1,0:T(8,128)(2,1)}, u32[]{:S(2)}) copy-start(bf16[4,2,4,144,128]{4,3,2,1,0:T(8,128)(2,1)} %get-tuple-element.29) | copy-start | bytes 3538948
  157.2 4.8 %collective-permute-start.16 = (bf16[2,4,2,4,144,128]{5,4,3,2,1,0:T(8,128)(2,1)}, bf16[2,4,2,4,144,128]{5,4,3,2,1,0:T(8,128)(2,1)S(1)}, u32[]{:S(2)}, u32[]{:S(2)}) collective-permute-start(bf16[2,4,2,4,144,128]{5,4,3,2,1,0:T(8,128)(2,1)} %get-tuple-element.28), channel_id=1, source_target_pairs={{0,1},{1,0},{2,3},{3,2},{4,5},{5,4},{6,7},{7,6},{8,9},{9,8},{10,11... | collective-permute-start | bytes 7077896 | tf_op jit(solution)/shard_map/ppermute | solution.py:36
  162.6 21.8 %collective-permute-start.18 = (bf16[4,2,4,72,128]{4,3,2,1,0:T(8,128)(2,1)S(1)}, bf16[4,2,4,72,128]{4,3,2,1,0:T(8,128)(2,1)S(1)}, u32[]{:S(2)}, u32[]{:S(2)}) collective-permute-start(bf16[4,2,4,72,128]{4,3,2,1,0:T(8,128)(2,1)S(1)} %slice.218), channel_id=1, source_target_pairs={{0,16},{1,17},{2,18},{3,19},{4,20},{5,21},{6,22},{7,23},{8,24},{9,... | collective-permute-start | bytes 1769480 | tf_op jit(solution)/shard_map/ppermute | solution.py:52
  162.8 32.3 %collective-permute-start.19 = (bf16[4,2,4,72,128]{4,3,2,1,0:T(8,128)(2,1)S(1)}, bf16[4,2,4,72,128]{4,3,2,1,0:T(8,128)(2,1)S(1)}, u32[]{:S(2)}, u32[]{:S(2)}) collective-permute-start(bf16[4,2,4,72,128]{4,3,2,1,0:T(8,128)(2,1)S(1)} %get-tuple-element.39), channel_id=1, source_target_pairs={{0,24},{1,25},{2,26},{3,27},{4,28},{5,29},{6,30},{7,31},{8,16},{9,... | collective-permute-start | bytes 1769480 | tf_op jit(solution)/shard_map/ppermute | solution.py:52
  162.9 32.4 %collective-permute-start.17 = (bf16[4,2,4,72,128]{4,3,2,1,0:T(8,128)(2,1)S(1)}, bf16[4,2,4,72,128]{4,3,2,1,0:T(8,128)(2,1)S(1)}, u32[]{:S(2)}, u32[]{:S(2)}) collective-permute-start(bf16[4,2,4,72,128]{4,3,2,1,0:T(8,128)(2,1)S(1)} %get-tuple-element.40), channel_id=1, source_target_pairs={{0,8},{1,9},{2,10},{3,11},{4,12},{5,13},{6,14},{7,15},{8,0},{9,1},... | collective-permute-start | bytes 1769480 | tf_op jit(solution)/shard_map/ppermute | solution.py:40
  202.5 17.2 %collective-permute-start.23 = (bf16[2,6,128,128]{3,2,1,0:T(8,128)(2,1)S(1)}, bf16[2,6,128,128]{3,2,1,0:T(8,128)(2,1)S(1)}, u32[]{:S(2)}, u32[]{:S(2)}) collective-permute-start(bf16[2,6,128,128]{3,2,1,0:T(8,128)(2,1)S(1)} %bitcast.57), channel_id=1, source_target_pairs={{0,8},{1,9},{2,10},{3,11},{4,12},{5,13},{6,14},{7,15},{8,0},{9,1},... | collective-permute-start | bytes 1179656 | tf_op jit(solution)/shard_map/ppermute | solution.py:40
  205.4 17.2 %copy-start.2 = (s32[4]{0:T(128)S(1)}, s32[4]{0:T(128)}, u32[]{:S(2)}) copy-start(s32[4]{0:T(128)} %pad_add_fusion.s_ref) | copy-start | bytes 52
  205.4 9.9 %collective-permute-start.22 = (bf16[2,4,144,128]{3,2,1,0:T(8,128)(2,1)S(1)}, bf16[2,4,144,128]{3,2,1,0:T(8,128)(2,1)S(1)}, u32[]{:S(2)}, u32[]{:S(2)}) collective-permute-start(bf16[2,4,144,128]{3,2,1,0:T(8,128)(2,1)S(1)} %get-tuple-element.35), channel_id=1, source_target_pairs={{0,2},{1,3},{2,4},{3,5},{4,6},{5,7},{6,0},{7,1},{8,10},{9,11},{10,... | collective-permute-start | bytes 884744 | tf_op jit(solution)/shard_map/ppermute | solution.py:44
  205.5 9.8 %collective-permute-start.20 = (bf16[2,4,144,128]{3,2,1,0:T(8,128)(2,1)S(1)}, bf16[2,4,144,128]{3,2,1,0:T(8,128)(2,1)S(1)}, u32[]{:S(2)}, u32[]{:S(2)}) collective-permute-start(bf16[2,4,144,128]{3,2,1,0:T(8,128)(2,1)S(1)} %get-tuple-element.36), channel_id=1, source_target_pairs={{0,6},{1,7},{2,0},{3,1},{4,2},{5,3},{6,4},{7,5},{8,14},{9,15},{10,... | collective-permute-start | bytes 884744 | tf_op jit(solution)/shard_map/ppermute | solution.py:44
  208.2 11.6 %collective-permute-start.21 = (bf16[2,4,144,128]{3,2,1,0:T(8,128)(2,1)S(1)}, bf16[2,4,144,128]{3,2,1,0:T(8,128)(2,1)S(1)}, u32[]{:S(2)}, u32[]{:S(2)}) collective-permute-start(bf16[2,4,144,128]{3,2,1,0:T(8,128)(2,1)S(1)} %get-tuple-element.37), channel_id=1, source_target_pairs={{0,4},{1,5},{2,6},{3,7},{4,0},{5,1},{6,2},{7,3},{8,12},{9,13},{10,... | collective-permute-start | bytes 884744 | tf_op jit(solution)/shard_map/ppermute | solution.py:44
  219.7 4.8 %copy-start.8 = (bf16[2,6,128,128]{3,2,1,0:T(8,128)(2,1)}, bf16[2,6,128,128]{3,2,1,0:T(8,128)(2,1)S(1)}, u32[]{:S(2)}) copy-start(bf16[2,6,128,128]{3,2,1,0:T(8,128)(2,1)S(1)} %collective-permute-done.23.c_ref) | copy-start | bytes 1179652
  219.8 7.2 %collective-permute-start.24 = (bf16[2,6,128,128]{3,2,1,0:T(8,128)(2,1)S(1)}, bf16[2,6,128,128]{3,2,1,0:T(8,128)(2,1)S(1)}, u32[]{:S(2)}, u32[]{:S(2)}) collective-permute-start(bf16[2,6,128,128]{3,2,1,0:T(8,128)(2,1)S(1)} %pad_maximum_fusion.11), channel_id=1, source_target_pairs={{0,1},{1,0},{2,3},{3,2},{4,5},{5,4},{6,7},{7,6},{8,9},{9,8},{10,11... | collective-permute-start | bytes 1179656 | tf_op jit(solution)/shard_map/ppermute | solution.py:36
  227.0 0.8 copy-start.9
Sparse Core Ops, SparseCore 0:
  40.7 49.0 all-gather.1
  157.3 43.5 reduce-scatter.1
